TPU v7x, 32 devices: a whole 2x2x4 slice. The times are simulated.
32 devices in a mesh: vir: 8 (over z, x), ph: 2 (over y), vec: 2 (over core).
Axes of the slice: x: 2, y: 2, z: 4, core: 2. Of those that a mesh axis runs over, the one named last changes fastest.
Arguments:
- vv_factor: bfloat16 [1024, 1024, 1024], P(('ph', 'vec'), 'vir'), may hold values from -0.1875 to 0.1875
- ladder_amp: bfloat16 [1024, 1024, 256], P(None, 'vir'), may hold values from -0.1875 to 0.1875
- cycle_amp: bfloat16 [1024, 32, 128], P(('vir', 'ph'), None, 'vec'), may hold values from -0.015625 to 0.015625
- ov_slots: bfloat16 [2048, 1024, 128], P(('vir', 'ph'), None, 'vec'), may hold values from -6 to 6
- owner_of: int32 [1024], P(('vir', 'ph')), may hold values from 0 to 1, as said below
- slot_of: int32 [1024], P(('vir', 'ph')), may hold values from 0 to 127, as said below
- ov_pairs: bfloat16 [1024, 8, 1024], P(('ph', 'vec'), None, 'vir'), may hold values from -0.1875 to 0.1875
- eps_vir: float32 [1024], replicated, may hold values from 0.5 to 3
- eps_occ: float32 [128], replicated, may hold values from -3 to -0.5
Outputs:
- residual: bfloat16 [1024, 256], P('vir', ('ph', 'vec'))
- update: float32 [1024, 256], P('vir', ('ph', 'vec'))
Inputs may be any that keep to these rules, and one draw needn't show every extreme that they name: `owner_of`: within each run of 128 consecutive blocks (one vir index) one owner holds exactly 128 blocks and no owner more. `slot_of`: distinct among the blocks of one run with the same owner.
All inputs are finite; a program needn't handle non-finite values.
Results may differ from a plain program's by a relative error of at most 0.0055.
Values may be sent and summed in bfloat16 or wider, within the bound.
No kernel may reach another device: no remote copies, remote signals or barrier semaphores. Data moves between devices by JAX's collectives and lax.ppermute only.
A program may use at most 320 MiB of HBM per device.

v0:
```python
import jax
import jax.numpy as jnp
from jax import lax
from jax.sharding import PartitionSpec as P


def local(
    vv_factor, ladder_amp, cycle_amp, ov_slots, owner_of, slot_of, ov_pairs, eps_vir, eps_occ
):
    chol_local, slab_width, virtuals = vv_factor.shape
    pair_count = ladder_amp.shape[2]
    row_piece = vv_factor[:, :, 0]
    factor_row = lax.all_gather(row_piece, "vir", axis=1, tiled=True)
    half = jnp.dot(
        factor_row,
        ladder_amp.reshape(virtuals, slab_width * pair_count),
        preferred_element_type=jnp.float32,
    )
    half = half.astype(jnp.bfloat16).reshape(chol_local * slab_width, pair_count)
    flat_factor = vv_factor.reshape(chol_local * slab_width, virtuals)
    block_local, occ_rows, block_part = cycle_amp.shape
    owner_total = lax.axis_size("ph")
    targets = owner_of[None, :] == jnp.arange(owner_total, dtype=jnp.int32)[:, None]
    outgoing = jnp.where(targets[:, :, None, None], cycle_amp[None], jnp.zeros((), jnp.bfloat16))
    places = jnp.where(targets, slot_of[None, :], 0)
    arrived, arrived_slots = (
        lax.all_to_all(outgoing, "ph", split_axis=0, concat_axis=0, tiled=True),
        lax.all_to_all(places, "ph", split_axis=0, concat_axis=0, tiled=True),
    )
    capacity = ov_slots.shape[0]
    picks = (
        arrived_slots.reshape(-1)[:, None] == jnp.arange(capacity, dtype=jnp.int32)[None, :]
    ).astype(jnp.bfloat16)
    arranged = jnp.einsum(
        "ns,niw->siw",
        picks,
        arrived.reshape(-1, occ_rows, block_part),
        preferred_element_type=jnp.float32,
    )
    arranged = arranged.astype(jnp.bfloat16)
    cycle_part = jnp.einsum("siw,spw->ip", arranged, ov_slots, preferred_element_type=jnp.float32)
    near_groups = lax.axis_size("ph") * lax.axis_size("vec")
    summed = lax.psum(cycle_part, ("vir", "ph", "vec"))
    vector_share = summed.shape[1] // near_groups
    own_share = lax.dynamic_slice_in_dim(
        summed, lax.axis_index(("ph", "vec")) * vector_share, vector_share, 1
    )
    coupling = own_share.astype(jnp.bfloat16)
    second_count = ov_pairs.shape[1]
    cycle_term = jnp.einsum("ip,pjb->bij", coupling, ov_pairs, preferred_element_type=jnp.float32)
    cycle_term = cycle_term.reshape(slab_width, occ_rows * second_count)
    slab_start = lax.axis_index("vir") * slab_width
    slab = (
        lax.psum_scatter(
            lax.dot_general(
                flat_factor, half, (((0,), (0,)), ((), ())), preferred_element_type=jnp.float32
            ),
            "vir",
            scatter_dimension=0,
            tiled=True,
        )
        + cycle_term
    )
    result = lax.psum_scatter(slab, ("ph", "vec"), scatter_dimension=1, tiled=True)
    residual = result.astype(jnp.bfloat16)
    share_width = result.shape[1]
    pair_index = lax.axis_index(("ph", "vec")) * share_width + jnp.arange(
        share_width, dtype=jnp.int32
    )
    occ_count = eps_occ.shape[0]
    occ_ids = jnp.arange(occ_count, dtype=jnp.int32)[None, :]
    first_occ = jnp.sum(
        jnp.where((pair_index // second_count)[:, None] == occ_ids, eps_occ[None, :], 0.0), 1
    )
    second_occ = jnp.sum(
        jnp.where((pair_index % second_count)[:, None] == occ_ids, eps_occ[None, :], 0.0), 1
    )
    slab_energy = lax.dynamic_slice_in_dim(eps_vir, slab_start, slab_width, 0)
    denominator = (eps_vir[0] + slab_energy)[:, None] - first_occ[None, :] - second_occ[None, :]
    update = residual.astype(jnp.float32) / denominator
    return (residual, update)


def solution(mesh):
    placed = (
        P(("ph", "vec"), "vir", None),
        P(None, "vir", None),
        P(("vir", "ph"), None, "vec"),
        P(("vir", "ph"), None, "vec"),
        P(("vir", "ph")),
        P(("vir", "ph")),
        P(("ph", "vec"), None, "vir"),
        P(),
        P(),
    )
    return jax.shard_map(
        local,
        mesh=mesh,
        in_specs=placed,
        out_specs=(P("vir", ("ph", "vec")), P("vir", ("ph", "vec"))),
        check_vma=False,
    )
```

profile of v0, /device:TPU:0, one launch (start us, length us, event | category | flops | bytes accessed | tf_op | source)
XLA Modules:
  0.0 299.5 jit_solution(14703549049964965735)
XLA Ops:
  7.2 59.4 %copy.34 = bf16[128,8,128,256]{3,1,2,0:T(8,128)(2,1)} copy(bf16[128,8,128,256]{3,2,1,0:T(8,128)(2,1)} %bitcast.9) | data formatting | bytes 134217728
  66.7 10.3 %slice.6 = bf16[256,128,1]{2,1,0:T(8,128)(2,1)} slice(bf16[256,128,1024]{2,1,0:T(8,128)(2,1)} %param.9), slice={[0:256], [0:128], [0:1]} | slice | bytes 131072 | tf_op jit(solution)/shard_map/slice | solution.py:12
  77.0 6.9 %copy.33 = bf16[256,128,1]{1,0,2:T(8,128)(2,1)S(1)} copy(bf16[256,128,1]{2,1,0:T(8,128)(2,1)} %slice.6) | data formatting | bytes 131072
  83.9 29.7 %all-gather = bf16[256,1024,1]{1,0,2:T(8,128)(2,1)S(1)} all-gather(bf16[256,128,1]{1,0,2:T(8,128)(2,1)S(1)} %copy.33), channel_id=2, replica_groups=mesh['vir'=8,'ph'=2,'vec'=2] {'vir'}, dimensions={1}, use_global_device_ids=true | all-gather | bytes 589824 | tf_op jit(solution)/shard_map/all_gather | solution.py:13
  113.6 30.6 %convolution_convert_fusion = bf16[256,32768]{1,0:T(8,128)(2,1)} fusion(bf16[1024,32768]{1,0:T(8,128)(2,1)} %bitcast.10, bf16[256,1024,1]{1,0,2:T(8,128)(2,1)S(1)} %all-gather), kind=kOutput, calls=%fused_computation | convolution fusion | flops 17188257792 | bytes 84410368 | tf_op jit(solution)/shard_map/dot_general | solution.py:14
  144.2 25.6 %reshape.125 = bf16[32768,256]{1,0:T(8,128)(2,1)} reshape(bf16[256,32768]{1,0:T(8,128)(2,1)} %convolution_convert_fusion) | data formatting | bytes 33554432 | tf_op jit(solution)/shard_map/reshape | solution.py:19
  169.8 31.4 %convolution_bitcast_fusion = f32[1024,256]{0,1:T(8,128)} fusion(bf16[32768,256]{1,0:T(8,128)(2,1)} %reshape.125, bf16[32768,1024]{1,0:T(8,128)(2,1)} %bitcast.1), kind=kOutput, calls=%fused_computation.1 | convolution fusion | flops 17179869184 | bytes 84934656 | tf_op jit(solution)/shard_map/dot_general | solution.py:55
  201.2 0.6 compare_select_fusion
  201.8 3.2 %all-to-all-start = ((s32[2,1,64]{2,1,0:T(1,128)}), s32[2,1,64]{2,1,0:T(1,128)S(1)}, u32[]{:S(2)}, u32[]{:S(2)}) async-start(s32[2,1,64]{2,1,0:T(1,128)} %compare_select_fusion), calls=%async_computation.1 | async-start | bytes 2048 | tf_op jit(solution)/shard_map/all_to_all | solution.py:28
  205.0 0.6 copy.28
  205.6 0.1 fusion.7
  205.7 1.5 reshape.144
  207.3 1.4 all-to-all-done
  208.7 3.5 %all-to-all-start.1 = ((bf16[2,2,65536]{2,1,0:T(2,128)(2,1)}), bf16[2,2,65536]{2,1,0:T(2,128)(2,1)S(1)}, u32[]{:S(2)}, u32[]{:S(2)}) async-start(bf16[2,2,65536]{2,1,0:T(2,128)(2,1)} %reshape.144), calls=%async_computation.2 | async-start | bytes 1048576 | tf_op jit(solution)/shard_map/all_to_all | solution.py:27
  212.1 0.3 reduce-scatter.5.cloned.1.call-start
  212.4 1.2 slice.7
  213.6 0.5 broadcast.132
  214.1 0.7 reduce.3
  214.9 3.8 %all-to-all-done.1 = bf16[2,2,65536]{2,1,0:T(2,128)(2,1)S(1)} async-done(((bf16[2,2,65536]{2,1,0:T(2,128)(2,1)}), bf16[2,2,65536]{2,1,0:T(2,128)(2,1)S(1)}, u32[]{:S(2)}, u32[]{:S(2)}) %all-to-all-start.1) | async-done | bytes 524320 | tf_op jit(solution)/shard_map/all_to_all | solution.py:27
  218.7 0.7 reshape.145
  219.4 1.1 copy.29
  220.5 0.5 reshape.130
  221.0 0.4 fusion.2
  221.5 1.6 copy.30
  223.1 7.2 %convolution_bitcast_fusion.2 = f32[32,1024]{1,0:T(8,128)S(1)} fusion(bf16[128,32,64]{2,1,0:T(8,128)(2,1)S(1)} %copy.30, bf16[128,1024,64]{1,2,0:T(8,128)(2,1)} %param.12), kind=kOutput, calls=%fused_computation.3 | convolution fusion | flops 536870912 | bytes 17432576 | tf_op jit(solution)/shard_map/siw,spw->ip/dot_general | solution.py:41
  230.3 39.2 %all-reduce.1 = bf16[32,1024]{1,0:T(8,128)(2,1)S(1)} all-reduce(f32[32,1024]{1,0:T(8,128)S(1)} %convolution_bitcast_fusion.2), channel_id=1, replica_groups=mesh['vir'=8,'ph'=2,'vec'=2] {'vir','ph','vec'}, use_global_device_ids=true, to_apply=%region_1.2 | all-reduce | flops 32768 | bytes 196608 | tf_op jit(solution)/shard_map/psum | solution.py:43
  269.6 0.2 convolution_bitcast_fusion.1
  269.8 1.6 bitcast_add_fusion
  271.4 1.4 dynamic-slice_add_fusion
  272.9 0.2 select_reduce_fusion.1
  273.1 18.2 %reduce-scatter.5.cloned.1.call-done = f32[128,64]{0,1:T(8,128)} async-done(((f32[128,256]{0,1:T(8,128)}), f32[128,64]{0,1:T(8,128)}) %reduce-scatter.5.cloned.1.call-update) | async-done | bytes 32784 | tf_op jit(solution)/shard_map/reduce_scatter | solution.py:64
  291.2 1.5 subtract_divide_fusion
  (18 shorter events, 0.3 us)
Async XLA Ops:
  7.2 262.4 %copy-start = (bf16[256,8,128]{2,1,0:T(8,128)(2,1)S(1)}, bf16[256,8,128]{2,1,0:T(8,128)(2,1)}, u32[]{:S(2)}) copy-start(bf16[256,8,128]{2,1,0:T(8,128)(2,1)} %param.15) | copy-start | bytes 1572868
  7.2 262.6 %reduce-scatter.3.cloned.1.call-start = ((), (), s32[]{:S(2)}) async-start(), calls=%async_computation.4 | async-start | bytes 1179648 | tf_op jit(solution)/shard_map/reduce_scatter | solution.py:54
  169.8 31.4 %copy-start.3 = (s32[64]{0:T(128)S(1)}, s32[64]{0:T(128)}, u32[]{:S(2)}) copy-start(s32[64]{0:T(128)} %param.14) | copy-start | bytes 772
  169.8 31.4 %copy-start.4 = (s32[64]{0:T(128)S(1)}, s32[64]{0:T(128)}, u32[]{:S(2)}) copy-start(s32[64]{0:T(128)} %param.13) | copy-start | bytes 772
  169.8 35.2 %copy-start.1 = (bf16[64,32,64]{2,1,0:T(8,128)(2,1)S(1)}, bf16[64,32,64]{2,1,0:T(8,128)(2,1)}, u32[]{:S(2)}) copy-start(bf16[64,32,64]{2,1,0:T(8,128)(2,1)} %param.11) | copy-start | bytes 786436
  201.8 6.9 %all-to-all-start = ((s32[2,1,64]{2,1,0:T(1,128)}), s32[2,1,64]{2,1,0:T(1,128)S(1)}, u32[]{:S(2)}, u32[]{:S(2)}) async-start(s32[2,1,64]{2,1,0:T(1,128)} %compare_select_fusion), calls=%async_computation.1 | async-start | bytes 2048 | tf_op jit(solution)/shard_map/all_to_all | solution.py:28
  208.7 10.1 %all-to-all-start.1 = ((bf16[2,2,65536]{2,1,0:T(2,128)(2,1)}), bf16[2,2,65536]{2,1,0:T(2,128)(2,1)S(1)}, u32[]{:S(2)}, u32[]{:S(2)}) async-start(bf16[2,2,65536]{2,1,0:T(2,128)(2,1)} %reshape.144), calls=%async_computation.2 | async-start | bytes 1048576 | tf_op jit(solution)/shard_map/all_to_all | solution.py:27
  212.1 79.1 %reduce-scatter.5.cloned.1.call-start = ((), (), s32[]{:S(2)}) async-start(), calls=%async_computation.5 | async-start | bytes 163840 | tf_op jit(solution)/shard_map/reduce_scatter | solution.py:64
  220.5 52.3 %copy-start.2 = (f32[128]{0:T(128)S(1)}, f32[128]{0:T(128)}, u32[]{:S(2)}) copy-start(f32[128]{0:T(128)} %param.17) | copy-start | bytes 1540
Sparse Core Ops, SparseCore 0:
  201.3 62.9 reduce-scatter.2
  271.6 19.6 reduce-scatter.4
where the time goes:
time: 301 us; the launch traced here: 300 us
  local copies, waits for them, and re-layouts  110 us (37%)
  matrix products  69.7 us (23%)
  blocking collectives  69 us (23%)
  waiting for transfers between devices  23.4 us (8%)
  between operations  14.2 us (5%)
  starting transfers between devices  6.98 us (2%)
  other arithmetic  6.12 us (2%)
    unnamed x16, local copies, waits for them, and re-layouts  69.7 us
    psum x1, blocking collectives, local(): summed = lax.psum(cycle_part, ('vir', 'ph', 'vec'))  39.2 us
    dot_general x1, matrix products, local(): lax.dot_general(flat_factor, half, (((0,), (0,)), ((), ())), preferred_el...  31.4 us
    dot_general x1, matrix products, local(): jnp.dot(factor_row, ladder_amp.reshape(virtuals, slab_width * pair_count)...  30.6 us
    all_gather x1, blocking collectives, local(): factor_row = lax.all_gather(row_piece, 'vir', axis=1, tiled=True)  29.7 us
    reshape x1, local copies, waits for them, and re-layouts, local(): half.astype(jnp.bfloat16).reshape(chol_local * slab_width, pair_count)  25.6 us
    reduce_scatter x1, waiting for transfers between devices, local(): lax.psum_scatter(slab, ('ph', 'vec'), scatter_dimension=1, tiled=True)  18.2 us
    slice x1, local copies, waits for them, and re-layouts, local(): row_piece = vv_factor[:, :, 0]  10.3 us
  transfers between devices with their start and end apart: 4, of which 3 were waited for; matrix products, arithmetic and copies ran while one was open for 6% of the time, Pallas kernels for 0%

commit v1 on v0

--- a/solution.py
+++ b/solution.py
@@ -1,10 +1,17 @@
+import functools
+
 import jax
 import jax.numpy as jnp
 from jax import lax
+from jax.experimental import pallas as pl
+from jax.experimental.pallas import tpu as pltpu
 from jax.sharding import PartitionSpec as P
 
-
-def local(
+LANES = 128
+bf16, f32 = jnp.bfloat16, jnp.float32
+
+
+def plain(
     vv_factor, ladder_amp, cycle_amp, ov_slots, owner_of, slot_of, ov_pairs, eps_vir, eps_occ
 ):
     chol_local, slab_width, virtuals = vv_factor.shape
@@ -81,6 +88,265 @@
     return (residual, update)
 
 
+def shifted(x, axes, k):
+    n = lax.axis_size(axes)
+    return lax.ppermute(x, axes, [(i, (i + k) % n) for i in range(n)])
+
+
+def round_robin(x, axes):
+    return [x] + [shifted(x, axes, k) for k in range(1, lax.axis_size(axes))]
+
+
+def row_kernel(x_ref, out_ref, acc):
+    step, rows = pl.program_id(1), x_ref.shape[0]
+    lane = lax.broadcasted_iota(jnp.int32, acc.shape, 1)
+
+    @pl.when(step == 0)
+    def _():
+        acc[...] = jnp.zeros_like(acc)
+
+    part = jnp.zeros(acc.shape, f32)
+    for p in range(rows):
+        column = x_ref[p].astype(f32)
+        part = jnp.where(lane == p, pltpu.roll(column, p, 1) if p else column, part)
+    part = pltpu.roll(part, step * rows, 1)
+    acc[...] = jnp.where(lane // rows == step, part, acc[...])
+
+    @pl.when(step == pl.num_programs(1) - 1)
+    def _():
+        out_ref[...] = acc[...].T.astype(bf16)
+
+
+def own_row(vv_factor):
+    chol, slab, _ = vv_factor.shape
+    rows = 32
+    steps = LANES // rows
+    return pl.pallas_call(
+        row_kernel,
+        grid=(chol // LANES, steps),
+        in_specs=[pl.BlockSpec((rows, slab, LANES), lambda g, k: (g * steps + k, 0, 0))],
+        out_specs=pl.BlockSpec((LANES, slab), lambda g, k: (g, 0)),
+        out_shape=jax.ShapeDtypeStruct((chol, slab), bf16),
+        scratch_shapes=[pltpu.VMEM((slab, LANES), f32)],
+        compiler_params=pltpu.CompilerParams(vmem_limit_bytes=16 << 20),
+        cost_estimate=pl.CostEstimate(
+            flops=2 * chol * slab * LANES, bytes_accessed=2 * chol * slab * LANES, transcendentals=0
+        ),
+    )(vv_factor)
+
+
+def cycle_kernel(shares, place_ref, code_ref, *refs):
+    (*amp_refs, ov_ref, out_ref, amps, acc, block_of) = refs
+    step = pl.program_id(0)
+    blocks, slots = code_ref.shape[0], block_of.shape[0]
+    own = amp_refs[0].shape[0]
+
+    @pl.when(step == 0)
+    def _():
+        for k, ref in enumerate(amp_refs):
+            amps[pl.ds(k * own, own)] = ref[...]
+        amps[blocks] = jnp.zeros(amps.shape[1:], bf16)
+        acc[...] = jnp.zeros_like(acc)
+        first = place_ref[0] * slots
+
+        @pl.loop(0, slots)
+        def _(s):
+            block_of[s] = blocks
+
+        @pl.loop(0, blocks)
+        def _(n):
+            slot = code_ref[n] - first
+
+            @pl.when((slot >= 0) & (slot < slots))
+            def _():
+                block_of[slot] = n
+
+    here, width, chol = ov_ref.shape
+    group = max(1, 256 // width)
+    total = acc[...]
+    for s in range(0, here, group):
+        left = jnp.concatenate([amps[block_of[step * here + s + q]] for q in range(group)], axis=1)
+        right = ov_ref[pl.ds(s, group)].reshape(group * width, chol)
+        total += jnp.dot(left, right, preferred_element_type=f32)
+    acc[...] = total
+
+    @pl.when(step == pl.num_programs(0) - 1)
+    def _():
+        share = chol // shares
+        for k in range(shares):
+            start = lax.rem(place_ref[1] + k, shares) * share
+            out_ref[k] = acc[:, pl.ds(pl.multiple_of(start, share), share)]
+
+
+def cycle_partial(cycle_amp, ov_slots, owner_of, slot_of):
+    slots, chol, width = ov_slots.shape
+    occ = cycle_amp.shape[1]
+    shares = lax.axis_size(("ph", "vec"))
+    codes = jnp.concatenate(round_robin(owner_of * slots + slot_of, "ph"))
+    amps = round_robin(cycle_amp, "ph")
+    place = jnp.stack([lax.axis_index("ph"), lax.axis_index(("ph", "vec"))]).astype(jnp.int32)
+    here = 16
+    whole = pl.BlockSpec(memory_space=pltpu.VMEM)
+    scalars = pl.BlockSpec(memory_space=pltpu.SMEM)
+    return pl.pallas_call(
+        functools.partial(cycle_kernel, shares),
+        grid=(slots // here,),
+        in_specs=[scalars, scalars]
+        + [whole] * len(amps)
+        + [pl.BlockSpec((here, width, chol), lambda i: (i, 0, 0))],
+        out_specs=pl.BlockSpec((shares, occ, chol // shares), lambda i: (0, 0, 0)),
+        out_shape=jax.ShapeDtypeStruct((shares, occ, chol // shares), f32),
+        scratch_shapes=[
+            pltpu.VMEM((codes.shape[0] + 1, occ, width), bf16),
+            pltpu.VMEM((occ, chol), f32),
+            pltpu.SMEM((slots,), jnp.int32),
+        ],
+        compiler_params=pltpu.CompilerParams(vmem_limit_bytes=24 << 20),
+        cost_estimate=pl.CostEstimate(
+            flops=2 * occ * slots * width * chol,
+            bytes_accessed=2 * slots * width * chol,
+            transcendentals=0,
+        ),
+    )(place, codes, *amps, jnp.swapaxes(ov_slots, 1, 2))
+
+
+def ladder_kernel(place_ref, *refs):
+    (*row_refs, amp_ref, factor_ref, out_ref, rows, turned, half, left, right) = refs
+    virtuals, deep, pairs = amp_ref.shape
+    chol, slab = row_refs[0].shape
+    count = len(row_refs)
+
+    @pl.when(pl.program_id(0) == 0)
+    def _():
+        out_ref[...] = jnp.zeros_like(out_ref)
+        for k, ref in enumerate(row_refs):
+            rows[lax.rem(place_ref[0] - k + count, count)] = ref[...]
+
+    tall = left.shape[0] // deep
+
+    @pl.loop(0, virtuals // tall)
+    def _(k):
+        for h, ref in enumerate((left, right)):
+            x = amp_ref[pl.ds(k * tall, tall), :, pl.ds(h * LANES, LANES)]
+            ref[...] = x.astype(f32).reshape(tall * deep, LANES)
+        for d in range(deep):
+            for h, ref in enumerate((left, right)):
+                turned[d, pl.ds(k * tall, tall), pl.ds(h * LANES, LANES)] = ref[
+                    pl.ds(d, tall, stride=deep), :
+                ].astype(bf16)
+
+    row = jnp.concatenate([rows[k] for k in range(count)], axis=1)
+    for d in range(deep):
+        product = jnp.dot(row, turned[d], preferred_element_type=f32)
+        for h in range(2):
+            half[h, pl.ds(d, chol, stride=deep), :] = product[:, h * LANES : (h + 1) * LANES]
+
+    step = 512
+
+    @pl.loop(0, chol * deep // step)
+    def _(k):
+        flat = jnp.concatenate([half[h, pl.ds(k * step, step), :] for h in range(2)], axis=1)
+        block = factor_ref[pl.ds(k * (step // deep), step // deep)]
+        out_ref[...] += lax.dot_general(
+            flat.astype(bf16),
+            block.reshape(step, block.shape[2]),
+            (((0,), (0,)), ((), ())),
+            preferred_element_type=f32,
+        )
+
+
+def ladder_partial(row_parts, ladder_amp, vv_factor):
+    virtuals, slab, pairs = ladder_amp.shape
+    chol = vv_factor.shape[0]
+    deep, tall = 16, 128
+    place = lax.axis_index("vir").astype(jnp.int32)[None]
+    return pl.pallas_call(
+        ladder_kernel,
+        grid=(slab // deep,),
+        in_specs=[pl.BlockSpec(memory_space=pltpu.SMEM)]
+        + [pl.BlockSpec(memory_space=pltpu.VMEM)] * len(row_parts)
+        + [
+            pl.BlockSpec((virtuals, deep, pairs), lambda i: (0, i, 0)),
+            pl.BlockSpec((chol, deep, virtuals), lambda i: (0, i, 0)),
+        ],
+        out_specs=pl.BlockSpec((pairs, virtuals), lambda i: (0, 0)),
+        out_shape=jax.ShapeDtypeStruct((pairs, virtuals), f32),
+        scratch_shapes=[
+            pltpu.VMEM((len(row_parts), chol, slab), bf16),
+            pltpu.VMEM((deep, virtuals, pairs), bf16),
+            pltpu.VMEM((2, chol * deep, LANES), f32),
+            pltpu.VMEM((tall * deep, LANES), f32),
+            pltpu.VMEM((tall * deep, LANES), f32),
+        ],
+        compiler_params=pltpu.CompilerParams(vmem_limit_bytes=60 << 20),
+        cost_estimate=pl.CostEstimate(
+            flops=4 * chol * virtuals * slab * pairs,
+            bytes_accessed=2 * virtuals * slab * (pairs + chol),
+            transcendentals=0,
+        ),
+    )(place, *row_parts, ladder_amp, vv_factor)
+
+
+def scatter_sum(x, axes):
+    n = lax.axis_size(axes)
+    me = lax.axis_index(axes)
+    total = lax.dynamic_index_in_dim(x, me, 0, keepdims=False)
+    sent = x.astype(bf16)
+    for k in range(1, n):
+        piece = lax.dynamic_index_in_dim(sent, (me + k) % n, 0, keepdims=False)
+        total = total + shifted(piece, axes, k).astype(f32)
+    return total
+
+
+def local(
+    vv_factor, ladder_amp, cycle_amp, ov_slots, owner_of, slot_of, ov_pairs, eps_vir, eps_occ
+):
+    chol, slab, virtuals = vv_factor.shape
+    pairs = ladder_amp.shape[2]
+    slots, _, width = ov_slots.shape
+    n_vir, n_ph, n_vec = (lax.axis_size(a) for a in ("vir", "ph", "vec"))
+    fits = slab == LANES and pairs == 2 * LANES and chol % LANES == 0 and slots % 16 == 0
+    if not fits or 256 % width:
+        return plain(
+            vv_factor, ladder_amp, cycle_amp, ov_slots, owner_of, slot_of, ov_pairs, eps_vir, eps_occ
+        )
+    row_parts = round_robin(own_row(vv_factor), "vir")
+    pieces = cycle_partial(cycle_amp, ov_slots, owner_of, slot_of)
+    occ = pieces.shape[1]
+    coupling = pieces[0]
+    for k in range(1, n_ph * n_vec):
+        coupling = coupling + shifted(pieces[k], ("ph", "vec"), k)
+    coupling = sum(round_robin(coupling, "vir")).astype(bf16)
+    second_count = ov_pairs.shape[1]
+    cycle_term = jnp.einsum("ip,pjb->ijb", coupling, ov_pairs, preferred_element_type=f32)
+    cycle_term = cycle_term.reshape(pairs, slab)
+
+    ladder = ladder_partial(row_parts, ladder_amp, vv_factor)
+    vir = lax.axis_index("vir")
+    share = pairs // (n_ph * n_vec)
+    own = jnp.arange(n_vir, dtype=jnp.int32)[None, :, None] == vir
+    total = ladder.reshape(pairs, n_vir, slab) + jnp.where(own, cycle_term[:, None, :], 0.0)
+    total = total.reshape(n_ph, n_vec, share, virtuals)
+    total = scatter_sum(jnp.swapaxes(total, 0, 1), "vec")
+    total = scatter_sum(total, "ph")
+    total = scatter_sum(jnp.swapaxes(total.reshape(share, n_vir, slab), 0, 1), "vir")
+
+    residual = total.T.astype(bf16)
+    place = lax.axis_index(("ph", "vec"))
+    pair_index = place * share + jnp.arange(share, dtype=jnp.int32)
+    occ_ids = jnp.arange(eps_occ.shape[0], dtype=jnp.int32)[None, :]
+    first_occ = jnp.sum(
+        jnp.where((pair_index // second_count)[:, None] == occ_ids, eps_occ[None, :], 0.0), 1
+    )
+    second_occ = jnp.sum(
+        jnp.where((pair_index % second_count)[:, None] == occ_ids, eps_occ[None, :], 0.0), 1
+    )
+    slab_energy = lax.dynamic_slice_in_dim(eps_vir, vir * slab, slab, 0)
+    denominator = (eps_vir[0] + slab_energy)[:, None] - first_occ[None, :] - second_occ[None, :]
+    update = residual.astype(f32) / denominator
+    return residual, update
+
+
 def solution(mesh):
     placed = (
         P(("ph", "vec"), "vir", None),

time: 301 us -> 219 us (0.73)
  Pallas kernels: 0 us -> 144 us
  local copies, waits for them, and re-layouts: 110 us -> 7.85 us
  matrix products: 69.7 us -> 0.19 us
  blocking collectives: 69 us -> 0 us
  starting transfers between devices: 6.98 us -> 42.4 us
  between operations: 14.2 us -> 1.07 us
  waiting for transfers between devices: 23.4 us -> 19 us
    pallas_call x0 -> x3, Pallas kernels: none -> 144 us  [the longest x1 130 us: ladder_partial(): pl.pallas_call(ladder_kernel, grid=(slab // deep,), in_specs=[pl.BlockSpe...]
    dot_general x4 -> x1, matrix products: 69.4 us -> 0.19 us  [local(): jnp.einsum('ip,pjb->ijb', coupling, ov_pairs, preferred_element_type=f32)]
    unnamed x16 -> x36, local copies, waits for them, and re-layouts: 69.7 us -> 5.91 us
    ppermute x0 -> x28, starting transfers between devices: none -> 42.4 us  [shifted(): return lax.ppermute(x, axes, [(i, (i + k) % n) for i in range(n)])]
    psum x1 -> x0, blocking collectives: 39.2 us -> none  [local(): summed = lax.psum(cycle_part, ('vir', 'ph', 'vec'))]
    all_gather x1 -> x0, blocking collectives: 29.7 us -> none  [local(): factor_row = lax.all_gather(row_piece, 'vir', axis=1, tiled=True)]
    reshape x1 -> x0, local copies, waits for them, and re-layouts: 25.6 us -> none  [local(): half.astype(jnp.bfloat16).reshape(chol_local * slab_width, pair_count)]
    ppermute x0 -> x28, waiting for transfers between devices: none -> 19 us  [shifted(): return lax.ppermute(x, axes, [(i, (i + k) % n) for i in range(n)])]
  transfers between devices with their start and end apart: 4 -> 28, of which waited for: 3 -> 6; matrix products, arithmetic and copies ran while one was open for 6% -> 1% of each run, Pallas kernels for 0% -> 63%
where the time goes in v1:
time: 219 us
  Pallas kernels  144 us (66%)
  starting transfers between devices  42.4 us (19%)
  waiting for transfers between devices  19 us (9%)
  local copies, waits for them, and re-layouts  7.85 us (4%)
  other arithmetic  3.96 us (2%)
    pallas_call x1, Pallas kernels, ladder_partial(): pl.pallas_call(ladder_kernel, grid=(slab // deep,), in_specs=[pl.BlockSpe...  130 us
    ppermute x28, starting transfers between devices, shifted(): return lax.ppermute(x, axes, [(i, (i + k) % n) for i in range(n)])  42.4 us
    ppermute x28, waiting for transfers between devices, shifted(): return lax.ppermute(x, axes, [(i, (i + k) % n) for i in range(n)])  19 us
    pallas_call x1, Pallas kernels, own_row(): pl.pallas_call(row_kernel, grid=(chol // LANES, steps), in_specs=[pl.Bloc...  7.46 us
    pallas_call x1, Pallas kernels, cycle_partial(): pl.pallas_call(functools.partial(cycle_kernel, shares), grid=(slots // he...  7.17 us
    unnamed x36, local copies, waits for them, and re-layouts  5.91 us
  transfers between devices with their start and end apart: 28, of which 6 were waited for; matrix products, arithmetic and copies ran while one was open for 1% of the time, Pallas kernels for 63%

profile of v1, /device:TPU:0, one launch (start us, length us, event | category | flops | bytes accessed | tf_op | source)
XLA Modules:
  0.0 218.6 jit_solution(13345292701405979509)
XLA Ops:
  0.7 7.5 %shard_map.104.refs_0_ = bf16[256,128]{1,0:T(8,128)(2,1)S(1)} custom-call(bf16[256,128,1024]{2,1,0:T(8,128)(2,1)} %refs_9_.1), custom_call_target="tpu_custom_call" | custom-call | flops 8388608 | bytes 8388608 | tf_op jit(solution)/shard_map/pallas_call | solution.py:124
  8.2 3.0 %collective-permute-start = (bf16[256,128]{1,0:T(8,128)(2,1)S(1)}, bf16[256,128]{1,0:T(8,128)(2,1)S(1)}, u32[]{:S(2)}, u32[]{:S(2)}) collective-permute-start(bf16[256,128]{1,0:T(8,128)(2,1)S(1)} %shard_map.104.refs_0_), channel_id=1, source_target_pairs={{0,4},{4,8},{8,12},{12,16},{16,20},{20,24},{24,28},{28,0},{1,5},{5... | collective-permute-start | bytes 196616 | tf_op jit(solution)/shard_map/ppermute | solution.py:93
  11.1 1.6 collective-permute-start.1
  12.7 1.5 collective-permute-start.8
  14.9 11.0 %collective-permute-done.7 = s32[64]{0:T(128)S(1)} collective-permute-done((s32[64]{0:T(128)S(1)}, s32[64]{0:T(128)S(1)}, u32[]{:S(2)}, u32[]{:S(2)}) %collective-permute-start.7) | collective-permute-done | bytes 288 | tf_op jit(solution)/shard_map/ppermute | solution.py:93
  26.0 5.8 %copy-done.1 = bf16[128,1024,64]{1,2,0:T(8,128)(2,1)S(1)} copy-done((bf16[128,1024,64]{1,2,0:T(8,128)(2,1)S(1)}, bf16[128,1024,64]{1,2,0:T(8,128)(2,1)}, u32[]{:S(2)}) %copy-start.1) | copy-done | bytes 16777240
  31.7 7.2 %shard_map.106 = f32[4,32,256]{2,1,0:T(8,128)S(1)} custom-call(s32[2]{0:T(128)S(1)} %pad_add_fusion.place_ref, s32[128]{0:T(128)S(1)} %pad_add_fusion.1.code_ref, bf16[64,32,64]{2,1,0:T(8,128)(2,1)S(1)} %copy-done.2, bf16[64,32,64]{2,1,0:T(8,128)(2,1)S(1)} %collective-permute-done.8.refs_1_, bf16[128,64,1024]{2,1,0:T(8,128)(2,1)S(1)} %bitcast.67), custom_call_target="tpu_custom_call" | custom-call | flops 536870912 | bytes 16777216 | tf_op jit(solution)/shard_map/pallas_call | solution.py:191
  38.9 1.6 collective-permute-start.10
  41.0 1.9 collective-permute-done.10
  42.9 2.6 %collective-permute-start.2 = (bf16[256,128]{1,0:T(8,128)(2,1)S(1)}, bf16[256,128]{1,0:T(8,128)(2,1)S(1)}, u32[]{:S(2)}, u32[]{:S(2)}) collective-permute-start(bf16[256,128]{1,0:T(8,128)(2,1)S(1)} %shard_map.104.refs_0_), channel_id=1, source_target_pairs={{0,12},{4,16},{8,20},{12,24},{16,28},{20,0},{24,4},{28,8},{1,13},{... | collective-permute-start | bytes 196616 | tf_op jit(solution)/shard_map/ppermute | solution.py:93
  45.5 1.2 collective-permute-start.3
  46.7 2.6 %collective-permute-start.4 = (bf16[256,128]{1,0:T(8,128)(2,1)S(1)}, bf16[256,128]{1,0:T(8,128)(2,1)S(1)}, u32[]{:S(2)}, u32[]{:S(2)}) collective-permute-start(bf16[256,128]{1,0:T(8,128)(2,1)S(1)} %shard_map.104.refs_0_), channel_id=1, source_target_pairs={{0,20},{4,24},{8,28},{12,0},{16,4},{20,8},{24,12},{28,16},{1,21},{... | collective-permute-start | bytes 196616 | tf_op jit(solution)/shard_map/ppermute | solution.py:93
  49.4 1.4 collective-permute-start.5
  50.8 1.4 collective-permute-start.6
  52.8 0.8 collective-permute-done.3.refs_4_
  53.7 3.8 %collective-permute-start.14 = (f32[32,256]{1,0:T(8,128)S(1)}, f32[32,256]{1,0:T(8,128)S(1)}, u32[]{:S(2)}, u32[]{:S(2)}) collective-permute-start(f32[32,256]{1,0:T(8,128)S(1)} %fusion.7), channel_id=1, source_target_pairs={{0,12},{4,16},{8,20},{12,24},{16,28},{20,0},{24,4},{28,8},{1,13},{... | collective-permute-start | bytes 98312 | tf_op jit(solution)/shard_map/ppermute | solution.py:93
  57.5 3.1 %collective-permute-start.15 = (f32[32,256]{1,0:T(8,128)S(1)}, f32[32,256]{1,0:T(8,128)S(1)}, u32[]{:S(2)}, u32[]{:S(2)}) collective-permute-start(f32[32,256]{1,0:T(8,128)S(1)} %fusion.7), channel_id=1, source_target_pairs={{0,16},{4,20},{8,24},{12,28},{16,0},{20,4},{24,8},{28,12},{1,17},{... | collective-permute-start | bytes 98312 | tf_op jit(solution)/shard_map/ppermute | solution.py:93
  60.6 1.0 collective-permute-start.16
  61.7 1.4 collective-permute-start.17
  63.1 1.5 collective-permute-start.18
  64.6 129.5 %shard_map.105 = f32[256,1024]{1,0:T(8,128)} custom-call(s32[1]{0:T(128)} %bitcast.place_ref, bf16[256,128]{1,0:T(8,128)(2,1)} %copy-done.3, bf16[256,128]{1,0:T(8,128)(2,1)} %copy-done.4, bf16[256,128]{1,0:T(8,128)(2,1)} %copy-done.5, bf16[256,128]{1,0:T(8,128)(2,1)} %copy-done.6, bf16[256,128]{1,0:T(8,128)(2,1)} %copy-done.7, bf16[256,128]{1,0:T(8,128)(2,1)} %copy-done.8, ...), custom_call_target="tpu_custom_call" | custom-call | flops 34359738368 | bytes 134217728 | tf_op jit(solution)/shard_map/pallas_call | solution.py:263
  194.8 1.4 select_add_fusion
  196.3 1.5 collective-permute-done.19
  197.9 1.9 collective-permute-start.20
  199.9 1.2 slice.19
  201.3 2.3 %collective-permute-done.20 = bf16[64,1024]{1,0:T(8,128)(2,1)S(1)} collective-permute-done((bf16[64,1024]{1,0:T(8,128)(2,1)S(1)}, bf16[64,1024]{1,0:T(8,128)(2,1)S(1)}, u32[]{:S(2)}, u32[]{:S(2)}) %collective-permute-start.20) | collective-permute-done | bytes 131104 | tf_op jit(solution)/shard_map/ppermute | solution.py:93
  205.1 1.4 dynamic-slice_add_fusion
  206.6 2.7 %collective-permute-start.23 = (bf16[64,128]{1,0:T(8,128)(2,1)S(1)}, bf16[64,128]{1,0:T(8,128)(2,1)S(1)}, u32[]{:S(2)}, u32[]{:S(2)}) collective-permute-start(bf16[64,128]{1,0:T(8,128)(2,1)S(1)} %bitcast.74), channel_id=1, source_target_pairs={{0,12},{4,16},{8,20},{12,24},{16,28},{20,0},{24,4},{28,8},{1,13},{... | collective-permute-start | bytes 49160 | tf_op jit(solution)/shard_map/ppermute | solution.py:93
  209.3 1.9 collective-permute-start.24
  211.8 2.0 collective-permute-start.26
  213.8 2.7 %collective-permute-start.27 = (bf16[64,128]{1,0:T(8,128)(2,1)S(1)}, bf16[64,128]{1,0:T(8,128)(2,1)S(1)}, u32[]{:S(2)}, u32[]{:S(2)}) collective-permute-start(bf16[64,128]{1,0:T(8,128)(2,1)S(1)} %bitcast.77), channel_id=1, source_target_pairs={{0,28},{4,0},{8,4},{12,8},{16,12},{20,16},{24,20},{28,24},{1,29},{... | collective-permute-start | bytes 49160 | tf_op jit(solution)/shard_map/ppermute | solution.py:93
  216.6 1.4 collective-permute-done.27
  (87 shorter events, 5.8 us)
Async XLA Ops:
  0.6 193.6 %copy-start = (bf16[256,8,128]{2,1,0:T(8,128)(2,1)S(1)}, bf16[256,8,128]{2,1,0:T(8,128)(2,1)}, u32[]{:S(2)}) copy-start(bf16[256,8,128]{2,1,0:T(8,128)(2,1)} %param.15) | copy-start | bytes 1572868
  8.1 56.4 %copy-start.3 = (bf16[256,128]{1,0:T(8,128)(2,1)}, bf16[256,128]{1,0:T(8,128)(2,1)S(1)}, u32[]{:S(2)}) copy-start(bf16[256,128]{1,0:T(8,128)(2,1)S(1)} %shard_map.104.refs_0_) | copy-start | bytes 196612
  8.2 41.2 %collective-permute-start = (bf16[256,128]{1,0:T(8,128)(2,1)S(1)}, bf16[256,128]{1,0:T(8,128)(2,1)S(1)}, u32[]{:S(2)}, u32[]{:S(2)}) collective-permute-start(bf16[256,128]{1,0:T(8,128)(2,1)S(1)} %shard_map.104.refs_0_), channel_id=1, source_target_pairs={{0,4},{4,8},{8,12},{12,16},{16,20},{20,24},{24,28},{28,0},{1,5},{5... | collective-permute-start | bytes 196616 | tf_op jit(solution)/shard_map/ppermute | solution.py:93
  11.1 39.6 %collective-permute-start.1 = (bf16[256,128]{1,0:T(8,128)(2,1)S(1)}, bf16[256,128]{1,0:T(8,128)(2,1)S(1)}, u32[]{:S(2)}, u32[]{:S(2)}) collective-permute-start(bf16[256,128]{1,0:T(8,128)(2,1)S(1)} %shard_map.104.refs_0_), channel_id=1, source_target_pairs={{0,8},{4,12},{8,16},{12,20},{16,24},{20,28},{24,0},{28,4},{1,9},{5... | collective-permute-start | bytes 196616 | tf_op jit(solution)/shard_map/ppermute | solution.py:93
  12.7 13.2 %collective-permute-start.8 = (bf16[64,32,64]{2,1,0:T(8,128)(2,1)S(1)}, bf16[64,32,64]{2,1,0:T(8,128)(2,1)S(1)}, u32[]{:S(2)}, u32[]{:S(2)}) collective-permute-start(bf16[64,32,64]{2,1,0:T(8,128)(2,1)S(1)} %copy-done.2), channel_id=1, source_target_pairs={{0,2},{2,0},{1,3},{3,1},{4,6},{6,4},{5,7},{7,5},{8,10},{10,8},{9,1... | collective-permute-start | bytes 786440 | tf_op jit(solution)/shard_map/ppermute | solution.py:93
  14.3 11.6 %collective-permute-start.7 = (s32[64]{0:T(128)S(1)}, s32[64]{0:T(128)S(1)}, u32[]{:S(2)}, u32[]{:S(2)}) collective-permute-start(s32[64]{0:T(128)S(1)} %multiply_add_fusion), channel_id=1, source_target_pairs={{0,2},{2,0},{1,3},{3,1},{4,6},{6,4},{5,7},{7,5},{8,10},{10,8},{9,1... | collective-permute-start | bytes 776 | tf_op jit(solution)/shard_map/ppermute | solution.py:93
  38.9 4.0 %collective-permute-start.10 = (f32[32,256]{1,0:T(8,128)S(1)}, f32[32,256]{1,0:T(8,128)S(1)}, u32[]{:S(2)}, u32[]{:S(2)}) collective-permute-start(f32[32,256]{1,0:T(8,128)S(1)} %get-tuple-element.15), channel_id=1, source_target_pairs={{0,2},{1,3},{2,0},{3,1},{4,6},{5,7},{6,4},{7,5},{8,10},{9,11},{10,... | collective-permute-start | bytes 98312 | tf_op jit(solution)/shard_map/ppermute | solution.py:93
  40.5 5.0 %collective-permute-start.11 = (f32[32,256]{1,0:T(8,128)S(1)}, f32[32,256]{1,0:T(8,128)S(1)}, u32[]{:S(2)}, u32[]{:S(2)}) collective-permute-start(f32[32,256]{1,0:T(8,128)S(1)} %get-tuple-element.14), channel_id=1, source_target_pairs={{0,3},{1,0},{2,1},{3,2},{4,7},{5,4},{6,5},{7,6},{8,11},{9,8},{10,9... | collective-permute-start | bytes 98312 | tf_op jit(solution)/shard_map/ppermute | solution.py:93
  40.5 6.2 %collective-permute-start.9 = (f32[32,256]{1,0:T(8,128)S(1)}, f32[32,256]{1,0:T(8,128)S(1)}, u32[]{:S(2)}, u32[]{:S(2)}) collective-permute-start(f32[32,256]{1,0:T(8,128)S(1)} %get-tuple-element.13), channel_id=1, source_target_pairs={{0,1},{1,2},{2,3},{3,0},{4,5},{5,6},{6,7},{7,4},{8,9},{9,10},{10,1... | collective-permute-start | bytes 98312 | tf_op jit(solution)/shard_map/ppermute | solution.py:93
  42.9 9.3 %collective-permute-start.2 = (bf16[256,128]{1,0:T(8,128)(2,1)S(1)}, bf16[256,128]{1,0:T(8,128)(2,1)S(1)}, u32[]{:S(2)}, u32[]{:S(2)}) collective-permute-start(bf16[256,128]{1,0:T(8,128)(2,1)S(1)} %shard_map.104.refs_0_), channel_id=1, source_target_pairs={{0,12},{4,16},{8,20},{12,24},{16,28},{20,0},{24,4},{28,8},{1,13},{... | collective-permute-start | bytes 196616 | tf_op jit(solution)/shard_map/ppermute | solution.py:93
  45.5 8.1 %collective-permute-start.3 = (bf16[256,128]{1,0:T(8,128)(2,1)S(1)}, bf16[256,128]{1,0:T(8,128)(2,1)S(1)}, u32[]{:S(2)}, u32[]{:S(2)}) collective-permute-start(bf16[256,128]{1,0:T(8,128)(2,1)S(1)} %shard_map.104.refs_0_), channel_id=1, source_target_pairs={{0,16},{4,20},{8,24},{12,28},{16,0},{20,4},{24,8},{28,12},{1,17},{... | collective-permute-start | bytes 196616 | tf_op jit(solution)/shard_map/ppermute | solution.py:93
  46.7 7.0 %collective-permute-start.4 = (bf16[256,128]{1,0:T(8,128)(2,1)S(1)}, bf16[256,128]{1,0:T(8,128)(2,1)S(1)}, u32[]{:S(2)}, u32[]{:S(2)}) collective-permute-start(bf16[256,128]{1,0:T(8,128)(2,1)S(1)} %shard_map.104.refs_0_), channel_id=1, source_target_pairs={{0,20},{4,24},{8,28},{12,0},{16,4},{20,8},{24,12},{28,16},{1,21},{... | collective-permute-start | bytes 196616 | tf_op jit(solution)/shard_map/ppermute | solution.py:93
  49.4 15.2 %copy-start.4 = (bf16[256,128]{1,0:T(8,128)(2,1)}, bf16[256,128]{1,0:T(8,128)(2,1)S(1)}, u32[]{:S(2)}) copy-start(bf16[256,128]{1,0:T(8,128)(2,1)S(1)} %collective-permute-done.refs_1_) | copy-start | bytes 196612
  49.4 8.2 %collective-permute-start.5 = (bf16[256,128]{1,0:T(8,128)(2,1)S(1)}, bf16[256,128]{1,0:T(8,128)(2,1)S(1)}, u32[]{:S(2)}, u32[]{:S(2)}) collective-permute-start(bf16[256,128]{1,0:T(8,128)(2,1)S(1)} %shard_map.104.refs_0_), channel_id=1, source_target_pairs={{0,24},{4,28},{8,0},{12,4},{16,8},{20,12},{24,16},{28,20},{1,25},{... | collective-permute-start | bytes 196616 | tf_op jit(solution)/shard_map/ppermute | solution.py:93
  50.8 9.8 %collective-permute-start.6 = (bf16[256,128]{1,0:T(8,128)(2,1)S(1)}, bf16[256,128]{1,0:T(8,128)(2,1)S(1)}, u32[]{:S(2)}, u32[]{:S(2)}) collective-permute-start(bf16[256,128]{1,0:T(8,128)(2,1)S(1)} %shard_map.104.refs_0_), channel_id=1, source_target_pairs={{0,28},{4,0},{8,4},{12,8},{16,12},{20,16},{24,20},{28,24},{1,29},{... | collective-permute-start | bytes 196616 | tf_op jit(solution)/shard_map/ppermute | solution.py:93
  52.2 9.5 %collective-permute-start.12 = (f32[32,256]{1,0:T(8,128)S(1)}, f32[32,256]{1,0:T(8,128)S(1)}, u32[]{:S(2)}, u32[]{:S(2)}) collective-permute-start(f32[32,256]{1,0:T(8,128)S(1)} %fusion.7), channel_id=1, source_target_pairs={{0,4},{4,8},{8,12},{12,16},{16,20},{20,24},{24,28},{28,0},{1,5},{5... | collective-permute-start | bytes 98312 | tf_op jit(solution)/shard_map/ppermute | solution.py:93
  53.6 9.4 %collective-permute-start.13 = (f32[32,256]{1,0:T(8,128)S(1)}, f32[32,256]{1,0:T(8,128)S(1)}, u32[]{:S(2)}, u32[]{:S(2)}) collective-permute-start(f32[32,256]{1,0:T(8,128)S(1)} %fusion.7), channel_id=1, source_target_pairs={{0,8},{4,12},{8,16},{12,20},{16,24},{20,28},{24,0},{28,4},{1,9},{5... | collective-permute-start | bytes 98312 | tf_op jit(solution)/shard_map/ppermute | solution.py:93
  53.7 140.5 %collective-permute-start.14 = (f32[32,256]{1,0:T(8,128)S(1)}, f32[32,256]{1,0:T(8,128)S(1)}, u32[]{:S(2)}, u32[]{:S(2)}) collective-permute-start(f32[32,256]{1,0:T(8,128)S(1)} %fusion.7), channel_id=1, source_target_pairs={{0,12},{4,16},{8,20},{12,24},{16,28},{20,0},{24,4},{28,8},{1,13},{... | collective-permute-start | bytes 98312 | tf_op jit(solution)/shard_map/ppermute | solution.py:93
  57.5 136.7 %collective-permute-start.15 = (f32[32,256]{1,0:T(8,128)S(1)}, f32[32,256]{1,0:T(8,128)S(1)}, u32[]{:S(2)}, u32[]{:S(2)}) collective-permute-start(f32[32,256]{1,0:T(8,128)S(1)} %fusion.7), channel_id=1, source_target_pairs={{0,16},{4,20},{8,24},{12,28},{16,0},{20,4},{24,8},{28,12},{1,17},{... | collective-permute-start | bytes 98312 | tf_op jit(solution)/shard_map/ppermute | solution.py:93
  60.6 133.6 %collective-permute-start.16 = (f32[32,256]{1,0:T(8,128)S(1)}, f32[32,256]{1,0:T(8,128)S(1)}, u32[]{:S(2)}, u32[]{:S(2)}) collective-permute-start(f32[32,256]{1,0:T(8,128)S(1)} %fusion.7), channel_id=1, source_target_pairs={{0,20},{4,24},{8,28},{12,0},{16,4},{20,8},{24,12},{28,16},{1,21},{... | collective-permute-start | bytes 98312 | tf_op jit(solution)/shard_map/ppermute | solution.py:93
  61.7 132.5 %collective-permute-start.17 = (f32[32,256]{1,0:T(8,128)S(1)}, f32[32,256]{1,0:T(8,128)S(1)}, u32[]{:S(2)}, u32[]{:S(2)}) collective-permute-start(f32[32,256]{1,0:T(8,128)S(1)} %fusion.7), channel_id=1, source_target_pairs={{0,24},{4,28},{8,0},{12,4},{16,8},{20,12},{24,16},{28,20},{1,25},{... | collective-permute-start | bytes 98312 | tf_op jit(solution)/shard_map/ppermute | solution.py:93
  63.1 131.2 %collective-permute-start.18 = (f32[32,256]{1,0:T(8,128)S(1)}, f32[32,256]{1,0:T(8,128)S(1)}, u32[]{:S(2)}, u32[]{:S(2)}) collective-permute-start(f32[32,256]{1,0:T(8,128)S(1)} %fusion.7), channel_id=1, source_target_pairs={{0,28},{4,0},{8,4},{12,8},{16,12},{20,16},{24,20},{28,24},{1,29},{... | collective-permute-start | bytes 98312 | tf_op jit(solution)/shard_map/ppermute | solution.py:93
  64.6 136.5 %copy-start.11 = (f32[128]{0:T(128)S(1)}, f32[128]{0:T(128)}, u32[]{:S(2)}) copy-start(f32[128]{0:T(128)} %param.17) | copy-start | bytes 1540
  196.2 1.6 collective-permute-start.19
  197.9 5.7 %collective-permute-start.20 = (bf16[64,1024]{1,0:T(8,128)(2,1)S(1)}, bf16[64,1024]{1,0:T(8,128)(2,1)S(1)}, u32[]{:S(2)}, u32[]{:S(2)}) collective-permute-start(bf16[64,1024]{1,0:T(8,128)(2,1)S(1)} %fusion.4), channel_id=1, source_target_pairs={{0,2},{2,0},{1,3},{3,1},{4,6},{6,4},{5,7},{7,5},{8,10},{10,8},{9,1... | collective-permute-start | bytes 393224 | tf_op jit(solution)/shard_map/ppermute | solution.py:93
  204.0 7.8 %collective-permute-start.21 = (bf16[64,128]{1,0:T(8,128)(2,1)S(1)}, bf16[64,128]{1,0:T(8,128)(2,1)S(1)}, u32[]{:S(2)}, u32[]{:S(2)}) collective-permute-start(bf16[64,128]{1,0:T(8,128)(2,1)S(1)} %bitcast.73), channel_id=1, source_target_pairs={{0,4},{4,8},{8,12},{12,16},{16,20},{20,24},{24,28},{28,0},{1,5},{5... | collective-permute-start | bytes 49160 | tf_op jit(solution)/shard_map/ppermute | solution.py:93
  204.4 9.3 %collective-permute-start.22 = (bf16[64,128]{1,0:T(8,128)(2,1)S(1)}, bf16[64,128]{1,0:T(8,128)(2,1)S(1)}, u32[]{:S(2)}, u32[]{:S(2)}) collective-permute-start(bf16[64,128]{1,0:T(8,128)(2,1)S(1)} %bitcast.72), channel_id=1, source_target_pairs={{0,8},{4,12},{8,16},{12,20},{16,24},{20,28},{24,0},{28,4},{1,9},{5... | collective-permute-start | bytes 49160 | tf_op jit(solution)/shard_map/ppermute | solution.py:93
  206.6 10.0 %collective-permute-start.23 = (bf16[64,128]{1,0:T(8,128)(2,1)S(1)}, bf16[64,128]{1,0:T(8,128)(2,1)S(1)}, u32[]{:S(2)}, u32[]{:S(2)}) collective-permute-start(bf16[64,128]{1,0:T(8,128)(2,1)S(1)} %bitcast.74), channel_id=1, source_target_pairs={{0,12},{4,16},{8,20},{12,24},{16,28},{20,0},{24,4},{28,8},{1,13},{... | collective-permute-start | bytes 49160 | tf_op jit(solution)/shard_map/ppermute | solution.py:93
  209.3 7.2 %collective-permute-start.24 = (bf16[64,128]{1,0:T(8,128)(2,1)S(1)}, bf16[64,128]{1,0:T(8,128)(2,1)S(1)}, u32[]{:S(2)}, u32[]{:S(2)}) collective-permute-start(bf16[64,128]{1,0:T(8,128)(2,1)S(1)} %bitcast.75), channel_id=1, source_target_pairs={{0,16},{4,20},{8,24},{12,28},{16,0},{20,4},{24,8},{28,12},{1,17},{... | collective-permute-start | bytes 49160 | tf_op jit(solution)/shard_map/ppermute | solution.py:93
  211.2 5.4 %collective-permute-start.25 = (bf16[64,128]{1,0:T(8,128)(2,1)S(1)}, bf16[64,128]{1,0:T(8,128)(2,1)S(1)}, u32[]{:S(2)}, u32[]{:S(2)}) collective-permute-start(bf16[64,128]{1,0:T(8,128)(2,1)S(1)} %bitcast.76), channel_id=1, source_target_pairs={{0,20},{4,24},{8,28},{12,0},{16,4},{20,8},{24,12},{28,16},{1,21},{... | collective-permute-start | bytes 49160 | tf_op jit(solution)/shard_map/ppermute | solution.py:93
  211.8 4.8 %collective-permute-start.26 = (bf16[64,128]{1,0:T(8,128)(2,1)S(1)}, bf16[64,128]{1,0:T(8,128)(2,1)S(1)}, u32[]{:S(2)}, u32[]{:S(2)}) collective-permute-start(bf16[64,128]{1,0:T(8,128)(2,1)S(1)} %bitcast.78), channel_id=1, source_target_pairs={{0,24},{4,28},{8,0},{12,4},{16,8},{20,12},{24,16},{28,20},{1,25},{... | collective-permute-start | bytes 49160 | tf_op jit(solution)/shard_map/ppermute | solution.py:93
  213.8 4.2 %collective-permute-start.27 = (bf16[64,128]{1,0:T(8,128)(2,1)S(1)}, bf16[64,128]{1,0:T(8,128)(2,1)S(1)}, u32[]{:S(2)}, u32[]{:S(2)}) collective-permute-start(bf16[64,128]{1,0:T(8,128)(2,1)S(1)} %bitcast.77), channel_id=1, source_target_pairs={{0,28},{4,0},{8,4},{12,8},{16,12},{20,16},{24,20},{28,24},{1,29},{... | collective-permute-start | bytes 49160 | tf_op jit(solution)/shard_map/ppermute | solution.py:93
  (10 other events, 104.2 us)
